TPU v7x, 128 devices: a whole 4x4x4 slice. The times are simulated.
128 devices in a mesh: coil: 4 (over z), slab: 32 (over y, x, core).
Axes of the slice: x: 4, y: 4, z: 4, core: 2. Of those that a mesh axis runs over, the one named last changes fastest.
Arguments:
- image: float32 [2, 256, 256, 256], P(None, 'slab'), may hold values from -6 to 6
- sens: float32 [4, 2, 256, 256, 256], P('coil', None, 'slab'), may hold values from -6 to 6
- weights: bfloat16 [8192, 128, 128], P('slab'), may hold values from -0.5 to 0.5
- bins: int32 [8192], P('slab'), may hold values from 0 to 4095
- counts: int32 [32], P('slab'), may hold values from 32 to 256, as said below
Outputs:
- result: float32 [2, 256, 256, 256], P(None, 'slab', 'coil')
Inputs may be any that keep to these rules, and one draw needn't show every extreme that they name: The two slabs at the middle of the second dimension hold 256 live tiles; counts fall towards the edges of k-space.
All inputs are finite; a program needn't handle non-finite values.
Results may differ from a plain program's by a relative error of at most 0.0003.
Values sent between devices are 32-bit elements; how exact they have to be, the bound alone decides.
A program may use at most 128 MiB of HBM per device.

v0:
```python
import functools

import numpy as np
import jax
import jax.numpy as jnp
import ml_dtypes
from jax import lax
from jax.experimental import pallas as pl
from jax.experimental.pallas import tpu as pltpu
from jax.sharding import PartitionSpec as P

N = 256
TILE = 128
SLOTS = 256
CHIPS = 16
RING = 4
PLANES = 8
VMEM_LIMIT = 56 * 1024 * 1024
F32 = jnp.float32
BF16 = jnp.bfloat16


def halves(values):
    high = values.astype(ml_dtypes.bfloat16)
    low = (values - high.astype(np.float64)).astype(ml_dtypes.bfloat16)
    return high, low


def tables():
    index = np.arange(N)
    angle = 2.0 * np.pi * (index[:, None] * index[None, :] % N) / N
    cosine, sine = np.cos(angle) / 16.0, np.sin(angle) / 16.0
    right = np.block([[cosine, -sine], [sine, cosine]])
    left = right.T
    packed = np.arange(2 * N).reshape(2, CHIPS, 2, 8)
    packed = packed.transpose(2, 1, 0, 3).reshape(-1)
    fwd_right = np.concatenate([halves(right)[k] for k in (0, 1, 0)], 0)
    fwd_left = np.concatenate([halves(left)[k] for k in (0, 1, 0)], 1)
    back_left = np.concatenate([halves(right[:, packed])[k] for k in (0, 1, 0)], 1)
    back_right = np.concatenate([halves(left)[k] for k in (0, 1, 0)], 0)
    lanes = []
    for chip in range(CHIPS):
        cos_x = np.repeat(cosine[:, chip * 16 : chip * 16 + 16], 8, axis=1)
        sin_x = np.repeat(sine[:, chip * 16 : chip * 16 + 16], 8, axis=1)
        cos_parts, sin_parts = halves(cos_x), halves(sin_x)
        lanes.append(np.concatenate([cos_parts[0], sin_parts[0], cos_parts[1], sin_parts[1]], 1))
    phases = np.stack(lanes)
    return fwd_right, fwd_left, back_left, back_right, phases, np.ascontiguousarray(phases.transpose(0, 2, 1))


def split(values):
    high = values.astype(BF16)
    low = (values - high.astype(F32)).astype(BF16)
    return high, low


def dot(a, b):
    return lax.dot_general(a, b, (((1,), (0,)), ((), ())), preferred_element_type=F32)


def forward_kernel(image, sens, right, left, out):
    image_re, image_im = image[0, 0], image[1, 0]
    sens_re, sens_im = sens[0, 0, 0], sens[0, 1, 0]
    field = jnp.concatenate(
        [sens_re * image_re - sens_im * image_im, sens_re * image_im + sens_im * image_re], 1
    )
    high, low = split(field)
    field = dot(jnp.concatenate([high, high, low], 1), right[...])
    high, low = split(jnp.concatenate([field[:, :N], field[:, N:]], 0))
    field = dot(left[...], jnp.concatenate([high, high, low], 0))
    field = field.reshape(2, CHIPS, 2, 8, N)
    for part in range(2):
        for core in range(2):
            out[core, :, part, 0] = field[part, :, core]


def forward(image, sens, right, left):
    return pl.pallas_call(
        forward_kernel,
        grid=(PLANES,),
        in_specs=[
            pl.BlockSpec((2, 1, N, N), lambda i: (0, i, 0, 0)),
            pl.BlockSpec((1, 2, 1, N, N), lambda i: (0, 0, i, 0, 0)),
            pl.BlockSpec((6 * N, 2 * N), lambda i: (0, 0)),
            pl.BlockSpec((2 * N, 6 * N), lambda i: (0, 0)),
        ],
        out_specs=pl.BlockSpec((2, CHIPS, 2, 1, 8, N), lambda i: (0, 0, 0, i, 0, 0)),
        out_shape=jax.ShapeDtypeStruct((2, CHIPS, 2, PLANES, 8, N), F32),
        compiler_params=pltpu.CompilerParams(vmem_limit_bytes=VMEM_LIMIT),
        cost_estimate=pl.CostEstimate(flops=6 * 2 * PLANES * 2 * N * 2 * N * N * 2, bytes_accessed=12 << 20, transcendentals=0),
    )(image, sens, right, left)


def place():
    slab = lax.axis_index("slab")
    core = lax.rem(slab, 2)
    chip = slab // 2
    x, y = lax.rem(chip, RING), chip // RING
    return core, chip, x, y


def device(x, y, core):
    return {"slab": (y * RING + x) * 2 + core}


def up(i, step=1):
    return lax.rem(i + step, RING)


def down(i):
    return lax.rem(i + RING - 1, RING)


def meet(peers):
    barrier = pltpu.get_barrier_semaphore()
    for peer in peers:
        pl.semaphore_signal(barrier, inc=1, device_id=peer, device_id_type=pl.DeviceIdType.MESH)
    pl.semaphore_wait(barrier, len(peers))


def remote(src, dst, send, recv, peer):
    return pltpu.make_async_remote_copy(
        src_ref=src, dst_ref=dst, send_sem=send, recv_sem=recv, device_id=peer, device_id_type=pl.DeviceIdType.MESH
    )


class RingSum:
    def __init__(self, src, via_up, via_down, from_down, from_up, send, recv, me, above, below):
        self.src, self.me = src, me
        rows = src.shape[1]
        self.half = (pl.ds(0, rows // 2), pl.ds(rows // 2, rows // 2))
        self.via_up, self.via_down, self.from_down, self.from_up = via_up, via_down, from_down, from_up
        first, second = self.half
        far, near_up, near_down = up(me, 2), up(me), down(me)
        self.copies = [
            remote(src.at[far, first], via_up, send.at[0], recv.at[0], above),
            remote(src.at[far, second], via_down, send.at[1], recv.at[1], below),
            remote(src.at[near_up, second], from_down.at[second], send.at[2], recv.at[2], above),
            remote(src.at[near_down, first], from_up.at[first], send.at[3], recv.at[3], below),
            remote(src.at[near_up, first], from_down.at[first], send.at[4], recv.at[4], above),
            remote(src.at[near_down, second], from_up.at[second], send.at[5], recv.at[5], below),
        ]

    def start(self):
        for copy in self.copies[:4]:
            copy.start()

    def relay(self):
        first, second = self.half
        self.copies[0].wait_recv()
        near = up(self.me)
        self.src[near, first] = self.src[near, first] + self.via_up[...]
        self.copies[4].start()
        self.copies[1].wait_recv()
        near = down(self.me)
        self.src[near, second] = self.src[near, second] + self.via_down[...]
        self.copies[5].start()

    def finish(self, out):
        for k in (2, 3, 4, 5):
            self.copies[k].wait_recv()
        out[...] = self.src[self.me] + self.from_down[...] + self.from_up[...]

    def drain(self):
        for copy in self.copies:
            copy.wait_send()


def scatter_kernel(
    field, bins_col, phases, out,
    both, table, part_a, part_b, mid_a, mid_b,
    va0, va1, va2, va3, vb0, vb1, vb2, vb3, wa0, wa1, wa2, wa3, wb0, wb1, wb2, wb3,
    local_sem, pair_send, pair_recv, send, recv,
):
    core, chip, x, y = place()
    sibling = device(x, y, 1 - core)
    right, left = device(up(x), y, core), device(down(x), y, core)
    above, below = device(x, up(y), core), device(x, down(y), core)
    own = pltpu.make_async_copy(field.at[core], both.at[core], local_sem.at[0])
    own.start()
    fetch = pltpu.make_async_copy(phases.at[chip], table, local_sem.at[1])
    fetch.start()
    meet([sibling, right, left, above, below])
    pair = [
        remote(field.at[1 - core, pl.ds(4 * k, 4)], both.at[core, pl.ds(4 * k, 4)], pair_send.at[k], pair_recv.at[k], sibling)
        for k in range(4)
    ]
    for copy in pair:
        copy.start()
    own.wait()
    fetch.wait()

    def slab_sums(p, carry):
        lane = lax.broadcasted_iota(jnp.int32, (SLOTS, 32), 1)
        bins = jnp.sum(jnp.where(lane == 2 * p + core, bins_col[...], 0.0), axis=1, keepdims=True).astype(jnp.int32)
        kx, ky, side = bins // 16, (bins // 2) % 8, bins % 2
        hot = jnp.where(lax.broadcasted_iota(jnp.int32, (SLOTS, N), 1) == kx, 1.0, 0.0).astype(BF16)
        phase = dot(hot, table[...])
        row = lax.broadcasted_iota(jnp.int32, (SLOTS, 4 * TILE), 1) % 8
        phase = jnp.where(row == ky, phase, 0.0).astype(BF16)
        mats = []
        for k in range(2):
            cosine, sine = phase[:, 2 * k * TILE : (2 * k + 1) * TILE], phase[:, (2 * k + 1) * TILE : (2 * k + 2) * TILE]
            mats.append(jnp.concatenate([jnp.concatenate([cosine, sine], 1), jnp.concatenate([-sine, cosine], 1)], 0))
        rows = jnp.concatenate(
            [both[0, p, 0].reshape(64, N), both[1, p, 0].reshape(64, N), both[0, p, 1].reshape(64, N), both[1, p, 1].reshape(64, N)], 0
        )
        high, low = split(rows)
        sums = dot(jnp.concatenate([mats[0], mats[1], mats[0]], 1), jnp.concatenate([high, high, low], 0))
        sums = jnp.where(jnp.concatenate([side, side], 0) == 0, sums[:, :TILE], sums[:, TILE:])
        px, py = p % RING, p // RING
        part_a[px, pl.ds(py * SLOTS, SLOTS)] = sums[:SLOTS]
        part_b[py, pl.ds(px * SLOTS, SLOTS)] = sums[SLOTS:]
        return carry

    for k in range(4):
        pair[k].wait_recv()
        lax.fori_loop(4 * k, 4 * k + 4, slab_sums, 0)

    a1 = RingSum(part_a, va0, va1, va2, va3, send.at[0], recv.at[0], x, right, left)
    b1 = RingSum(part_b, vb0, vb1, vb2, vb3, send.at[1], recv.at[1], y, above, below)
    a2 = RingSum(mid_a, wa0, wa1, wa2, wa3, send.at[2], recv.at[2], y, above, below)
    b2 = RingSum(mid_b, wb0, wb1, wb2, wb3, send.at[3], recv.at[3], x, right, left)
    a1.start()
    b1.start()
    a1.relay()
    b1.relay()
    a1.finish(part_a.at[x])
    for k in range(RING):
        mid_a[k] = part_a[x, pl.ds(k * SLOTS, SLOTS)]
    a2.start()
    b1.finish(part_b.at[y])
    for k in range(RING):
        mid_b[k] = part_b[y, pl.ds(k * SLOTS, SLOTS)]
    b2.start()
    a2.relay()
    b2.relay()
    a2.finish(out.at[0])
    b2.finish(out.at[1])
    for ring in (a1, b1, a2, b2):
        ring.drain()
    for copy in pair:
        copy.wait_send()


def scatter(field, bins_col, phases):
    big, small = RING * SLOTS, SLOTS
    vias = []
    for rows in (big, big, small, small):
        vias += [pltpu.VMEM((rows // 2, TILE), F32)] * 2 + [pltpu.VMEM((rows, TILE), F32)] * 2
    return pl.pallas_call(
        scatter_kernel,
        out_shape=jax.ShapeDtypeStruct((2, SLOTS, TILE), F32),
        in_specs=[
            pl.BlockSpec(memory_space=pl.ANY),
            pl.BlockSpec(memory_space=pltpu.VMEM),
            pl.BlockSpec(memory_space=pl.ANY),
        ],
        out_specs=pl.BlockSpec(memory_space=pltpu.VMEM),
        scratch_shapes=[
            pltpu.VMEM((2, CHIPS, 2, PLANES, 8, N), F32),
            pltpu.VMEM((N, 4 * TILE), BF16),
            pltpu.VMEM((RING, big, TILE), F32),
            pltpu.VMEM((RING, big, TILE), F32),
            pltpu.VMEM((RING, small, TILE), F32),
            pltpu.VMEM((RING, small, TILE), F32),
        ]
        + vias
        + [
            pltpu.SemaphoreType.DMA((2,)),
            pltpu.SemaphoreType.DMA((4,)),
            pltpu.SemaphoreType.DMA((4,)),
            pltpu.SemaphoreType.DMA((4, 6)),
            pltpu.SemaphoreType.DMA((4, 6)),
        ],
        compiler_params=pltpu.CompilerParams(collective_id=0, has_side_effects=True, vmem_limit_bytes=VMEM_LIMIT),
    )(field, bins_col, phases)


GROUP = 32


def grid_kernel(live, tiles, weights, out):
    row = lax.broadcasted_iota(jnp.int32, (32, TILE), 0) % 8
    base = pl.program_id(0) * GROUP
    for g in range(GROUP // 8):
        rows = pl.ds(8 * g, 8)
        high, low = split(jnp.concatenate([tiles[0, rows], tiles[1, rows]], 0))
        mat = weights[rows].reshape(8 * TILE, TILE)
        spread = lax.dot_general(
            jnp.concatenate([high, low], 0), mat, (((1,), (1,)), ((), ())), preferred_element_type=F32
        )
        samples = jnp.zeros((32, TILE), F32)
        for j in range(8):
            samples = jnp.where(row == j, spread[:, j * TILE : (j + 1) * TILE], samples)
        samples = samples[:16] + samples[16:]
        high = samples.astype(BF16).astype(F32)
        both = jnp.concatenate([high, samples - high], 0)
        masked = jnp.concatenate([jnp.where(row == j, both, 0.0).astype(BF16) for j in range(8)], 1)
        back = dot(masked, mat)
        back = back[:16] + back[16:]
        slot = base + 8 * g + lax.broadcasted_iota(jnp.int32, (16, TILE), 0) % 8
        back = jnp.where(slot < live[0], back, 0.0)
        out[0, rows] = back[:8]
        out[1, rows] = back[8:]


def grid(live, tiles, weights):
    return pl.pallas_call(
        grid_kernel,
        grid=(SLOTS // GROUP,),
        in_specs=[
            pl.BlockSpec(memory_space=pltpu.SMEM),
            pl.BlockSpec((2, GROUP, TILE), lambda i: (0, i, 0)),
            pl.BlockSpec((GROUP, TILE, TILE), lambda i: (i, 0, 0)),
        ],
        out_specs=pl.BlockSpec((2, GROUP, TILE), lambda i: (0, i, 0)),
        out_shape=jax.ShapeDtypeStruct((2, SLOTS, TILE), F32),
        compiler_params=pltpu.CompilerParams(vmem_limit_bytes=VMEM_LIMIT),
    )(live, tiles, weights)


class RingGather:
    def __init__(self, buf, send, recv, me, above, below):
        rows = buf.shape[1]
        first, second = pl.ds(0, rows // 2), pl.ds(rows // 2, rows // 2)
        near_down, near_up, far = down(me), up(me), up(me, 2)
        self.copies = [
            remote(buf.at[me], buf.at[me], send.at[0], recv.at[0], above),
            remote(buf.at[me], buf.at[me], send.at[1], recv.at[1], below),
            remote(buf.at[near_down, first], buf.at[near_down, first], send.at[2], recv.at[2], above),
            remote(buf.at[near_up, second], buf.at[near_up, second], send.at[3], recv.at[3], below),
        ]

    def start(self):
        self.copies[0].start()
        self.copies[1].start()

    def relay(self):
        self.copies[0].wait_recv()
        self.copies[2].start()
        self.copies[1].wait_recv()
        self.copies[3].start()

    def finish(self):
        self.copies[2].wait_recv()
        self.copies[3].wait_recv()

    def drain(self):
        for copy in self.copies:
            copy.wait_send()


def gather_kernel(
    back, bins_row, bins_col, phases, left, right, sens, out,
    all_a, all_b, mid_a, mid_b, table, sens_buf, plane, outgoing, term, via_up, via_down, from_down, from_up,
    local_sem, send, recv, pair_send, pair_recv, coil_send, coil_recv,
):
    core, chip, x, y = place()
    coil = lax.axis_index("coil")
    sibling = device(x, y, 1 - core)
    east, west = device(up(x), y, core), device(down(x), y, core)
    north, south = device(x, up(y), core), device(x, down(y), core)
    over, under = {"coil": up(coil)}, {"coil": down(coil)}
    fetch = pltpu.make_async_copy(phases.at[chip], table, local_sem.at[0])
    fetch.start()
    fetch_sens = pltpu.make_async_copy(sens.at[0], sens_buf, local_sem.at[1])
    fetch_sens.start()
    mid_a[y] = back[0]
    mid_b[x] = back[1]
    meet([sibling, east, west, north, south, over, under])

    a1 = RingGather(mid_a, send.at[0], recv.at[0], y, north, south)
    b1 = RingGather(mid_b, send.at[1], recv.at[1], x, east, west)
    a2 = RingGather(all_a, send.at[2], recv.at[2], x, east, west)
    b2 = RingGather(all_b, send.at[3], recv.at[3], y, north, south)
    a1.start()
    b1.start()
    a1.relay()
    b1.relay()
    a1.finish()
    for k in range(RING):
        all_a[x, pl.ds(k * SLOTS, SLOTS)] = mid_a[k]
    a2.start()
    b1.finish()
    for k in range(RING):
        all_b[y, pl.ds(k * SLOTS, SLOTS)] = mid_b[k]
    b2.start()
    a2.relay()
    b2.relay()
    fetch.wait()
    a2.finish()
    b2.finish()

    def slab_sums(p, carry):
        lane = lax.broadcasted_iota(jnp.int32, (SLOTS, 32), 1)
        column = jnp.sum(jnp.where(lane == 2 * p + core, bins_col[...], 0.0), axis=1, keepdims=True).astype(jnp.int32)
        side = column % 2
        bins = bins_row[pl.ds(2 * p + core, 1), :].astype(jnp.int32)
        kx, ky = bins // 16, (bins // 2) % 8
        hot = jnp.where(lax.broadcasted_iota(jnp.int32, (N, SLOTS), 0) == kx, 1.0, 0.0).astype(BF16)
        phase = dot(table[...], hot)
        row = lax.broadcasted_iota(jnp.int32, (4 * TILE, SLOTS), 0) % 8
        phase = jnp.where(row == ky, phase, 0.0).astype(BF16)
        mats = []
        for k in range(2):
            cosine, sine = phase[2 * k * TILE : (2 * k + 1) * TILE], phase[(2 * k + 1) * TILE : (2 * k + 2) * TILE]
            mats.append(jnp.concatenate([jnp.concatenate([cosine, -sine], 1), jnp.concatenate([sine, cosine], 1)], 0))
        px, py = p % RING, p // RING
        tiles = jnp.concatenate([all_a[px, pl.ds(py * SLOTS, SLOTS)], all_b[py, pl.ds(px * SLOTS, SLOTS)]], 0)
        side = jnp.concatenate([side, side], 0)
        tiles = jnp.concatenate([jnp.where(side == 0, tiles, 0.0), jnp.where(side == 1, tiles, 0.0)], 1)
        high, low = split(tiles)
        sums = dot(jnp.concatenate([mats[0], mats[1], mats[0]], 1), jnp.concatenate([high, high, low], 0))
        sums = sums.reshape(2, 2, PLANES, 8, N)
        lower, upper = sums[:, 0], sums[:, 1]
        mine = jnp.where(core == 0, lower, upper)
        other = jnp.where(core == 0, upper, lower)
        for part in range(2):
            plane[:, core, p, part] = mine[part]
            outgoing[:, p, part] = other[part]
        return carry

    lax.fori_loop(0, CHIPS, slab_sums, 0)
    pair = [remote(outgoing.at[i], plane.at[i, core], pair_send.at[i], pair_recv.at[i], sibling) for i in range(PLANES)]
    for copy in pair:
        copy.start()
    fetch_sens.wait()

    far, near_up, near_down = up(coil, 2), up(coil), down(coil)

    def coil_copies(i):
        s, r = coil_send.at[i], coil_recv.at[i]
        return [
            remote(term.at[i, far, 0], via_up.at[i], s.at[0], r.at[0], over),
            remote(term.at[i, far, 1], via_down.at[i], s.at[1], r.at[1], under),
            remote(term.at[i, near_up, 1], from_down.at[i, 1], s.at[2], r.at[2], over),
            remote(term.at[i, near_down, 0], from_up.at[i, 0], s.at[3], r.at[3], under),
            remote(term.at[i, near_up, 0], from_down.at[i, 0], s.at[4], r.at[4], over),
            remote(term.at[i, near_down, 1], from_up.at[i, 1], s.at[5], r.at[5], under),
        ]

    def relay(i):
        copies = coil_copies(i)
        copies[0].wait_recv()
        term[i, near_up, 0] = term[i, near_up, 0] + via_up[i]
        copies[4].start()
        copies[1].wait_recv()
        term[i, near_down, 1] = term[i, near_down, 1] + via_down[i]
        copies[5].start()

    def plane_back(i, carry):
        remote(outgoing.at[i], plane.at[i, core], pair_send.at[i], pair_recv.at[i], sibling).wait_recv()
        high, low = split(plane[i].reshape(2 * N, N))
        field = dot(left[...], jnp.concatenate([high, high, low], 0))
        high, low = split(jnp.concatenate([field[:N], field[N:]], 1))
        field = dot(jnp.concatenate([high, high, low], 1), right[...])
        field_re, field_im = field[:, :N], field[:, N:]
        sens_re, sens_im = sens_buf[0, i], sens_buf[1, i]
        term[i, :, 0] = (sens_re * field_re + sens_im * field_im).reshape(RING, N // RING, N)
        term[i, :, 1] = (sens_re * field_im - sens_im * field_re).reshape(RING, N // RING, N)
        for copy in coil_copies(i)[:4]:
            copy.start()

        @pl.when(i > 0)
        def _():
            relay(i - 1)

        return carry

    lax.fori_loop(0, PLANES, plane_back, 0)
    relay(PLANES - 1)

    def collect(i, carry):
        copies = coil_copies(i)
        for k in (2, 3, 4, 5):
            copies[k].wait_recv()
        total = term[i, coil] + from_down[i] + from_up[i]
        for part in range(2):
            out[part, i] = total[part]
        for copy in copies:
            copy.wait_send()
        return carry

    lax.fori_loop(0, PLANES, collect, 0)
    for ring in (a1, b1, a2, b2):
        ring.drain()
    for copy in pair:
        copy.wait_send()


def gather(back, bins_row, bins_col, phases, left, right, sens):
    quarter = N // RING
    vmem = pl.BlockSpec(memory_space=pltpu.VMEM)
    hbm = pl.BlockSpec(memory_space=pl.ANY)
    return pl.pallas_call(
        gather_kernel,
        out_shape=jax.ShapeDtypeStruct((2, PLANES, quarter, N), F32),
        in_specs=[vmem, vmem, vmem, hbm, vmem, vmem, hbm],
        out_specs=vmem,
        scratch_shapes=[
            pltpu.VMEM((RING, RING * SLOTS, TILE), F32),
            pltpu.VMEM((RING, RING * SLOTS, TILE), F32),
            pltpu.VMEM((RING, SLOTS, TILE), F32),
            pltpu.VMEM((RING, SLOTS, TILE), F32),
            pltpu.VMEM((4 * TILE, N), BF16),
            pltpu.VMEM((2, PLANES, N, N), F32),
            pltpu.VMEM((PLANES, 2, CHIPS, 2, 8, N), F32),
            pltpu.VMEM((PLANES, CHIPS, 2, 8, N), F32),
            pltpu.VMEM((PLANES, RING, 2, quarter, N), F32),
            pltpu.VMEM((PLANES, quarter, N), F32),
            pltpu.VMEM((PLANES, quarter, N), F32),
            pltpu.VMEM((PLANES, 2, quarter, N), F32),
            pltpu.VMEM((PLANES, 2, quarter, N), F32),
            pltpu.SemaphoreType.DMA((2,)),
            pltpu.SemaphoreType.DMA((4, 4)),
            pltpu.SemaphoreType.DMA((4, 4)),
            pltpu.SemaphoreType.DMA((PLANES,)),
            pltpu.SemaphoreType.DMA((PLANES,)),
            pltpu.SemaphoreType.DMA((PLANES, 6)),
            pltpu.SemaphoreType.DMA((PLANES, 6)),
        ],
        compiler_params=pltpu.CompilerParams(collective_id=1, has_side_effects=True, vmem_limit_bytes=VMEM_LIMIT),
    )(back, bins_row, bins_col, phases, left, right, sens)


def body(image, sens, weights, bins, counts):
    fwd_right, fwd_left, back_left, back_right, phases, phases_t = (jnp.asarray(t) for t in tables())
    bins_row = lax.all_gather(bins, "slab").astype(F32)
    bins_col = bins_row.T
    field = forward(image, sens, fwd_right, fwd_left)
    tiles = scatter(field, bins_col, phases)
    back = grid(counts, tiles, weights)
    return gather(back, bins_row, bins_col, phases_t, back_left, back_right, sens)


def solution(mesh):
    in_specs = (
        P(None, "slab", None, None),
        P("coil", None, "slab", None, None),
        P("slab", None, None),
        P("slab"),
        P("slab"),
    )
    out_specs = P(None, "slab", "coil", None)
    return jax.shard_map(body, mesh=mesh, in_specs=in_specs, out_specs=out_specs, check_vma=False)
```

profile of v0, /device:TPU:1, one launch (start us, length us, event | category | flops | bytes accessed | tf_op | source)
XLA Modules:
  0.0 186.9 jit_solution(9890067261296035731)
XLA Ops:
  0.7 25.8 %all-gather.1 = s32[32,1,256]{2,1,0:T(1,128)S(1)} all-gather(s32[1,1,256]{2,1,0:T(1,128)} %bitcast.6), channel_id=2, replica_groups=mesh['coil'=4,'slab'=32] {'slab'}, dimensions={0}, use_global_device_ids=true | all-gather | bytes 33792 | tf_op jit(solution)/shard_map/all_gather | solution.py:529
  26.4 0.1 copy.15
  26.5 0.7 convert_bitcast_fusion.1
  27.2 0.7 copy.16.bins_row
  27.9 13.1 %shard_map.109.field = f32[2,16,2,8,8,256]{5,4,3,2,1,0:T(8,128)} custom-call(f32[2,8,256,256]{3,2,1,0:T(8,128)} %image.1, f32[1,2,8,256,256]{4,3,2,1,0:T(8,128)} %sens.3, bf16[1536,512]{1,0:T(8,128)(2,1)} %constant.12.clone.right, bf16[512,1536]{1,0:T(8,128)(2,1)} %constant.13.clone.left), custom_call_target="tpu_custom_call" | custom-call | flops 12884901888 | bytes 12582912 | tf_op jit(solution)/shard_map/pallas_call | solution.py:78
  41.0 44.8 %shard_map.110.tiles = f32[2,256,128]{2,1,0:T(8,128)} custom-call(f32[2,16,2,8,8,256]{5,4,3,2,1,0:T(8,128)} %shard_map.109.field, f32[256,32]{1,0:T(8,128)} %get-tuple-element.6.bins_col, bf16[16,256,512]{2,1,0:T(8,128)(2,1)} %constant.16.clone.phases), custom_call_target="tpu_custom_call" | custom-call | tf_op jit(solution)/shard_map/pallas_call | solution.py:251
  85.8 11.1 %shard_map.111.back = f32[2,256,128]{2,1,0:T(8,128)} custom-call(s32[1]{0:T(128)S(6)} %copy.18.live, f32[2,256,128]{2,1,0:T(8,128)} %shard_map.110.tiles, bf16[256,128,128]{2,1,0:T(8,128)(2,1)} %weights.1), custom_call_target="tpu_custom_call" | custom-call | tf_op jit(solution)/shard_map/pallas_call | solution.py:309
  96.9 87.7 %shard_map.112 = f32[2,8,64,256]{3,2,1,0:T(8,128)} custom-call(f32[2,256,128]{2,1,0:T(8,128)} %shard_map.111.back, f32[32,256]{1,0:T(8,128)} %copy.16.bins_row, f32[256,32]{1,0:T(8,128)} %get-tuple-element.6.bins_col, bf16[16,512,256]{2,1,0:T(8,128)(2,1)} %constant.17.clone.phases, bf16[512,1536]{1,0:T(8,128)(2,1)} %constant.14.clone.left, ...), custom_call_target="tpu_custom_call" | custom-call | tf_op jit(solution)/shard_map/pallas_call | solution.py:496
  184.6 2.3 %copy.19 = f32[2,8,64,256]{3,2,1,0:T(8,128)} copy(f32[2,8,64,256]{3,2,1,0:T(8,128)} %shard_map.112) | data formatting | bytes 2097152
where the time goes:
time: 188 us; the launch traced here: 187 us
  Pallas kernels  157 us (84%)
  blocking collectives  25.8 us (14%)
  local copies, waits for them, and re-layouts  3.09 us (2%)
    pallas_call x1, Pallas kernels, gather(): pl.pallas_call(gather_kernel, out_shape=jax.ShapeDtypeStruct((2, PLANES,...  87.7 us
    pallas_call x1, Pallas kernels, scatter(): pl.pallas_call(scatter_kernel, out_shape=jax.ShapeDtypeStruct((2, SLOTS,...  44.8 us
    all_gather x1, blocking collectives, body(): bins_row = lax.all_gather(bins, 'slab').astype(F32)  25.8 us
    pallas_call x1, Pallas kernels, forward(): pl.pallas_call(forward_kernel, grid=(PLANES,), in_specs=[pl.BlockSpec((2,...  13.1 us
    pallas_call x1, Pallas kernels, grid(): pl.pallas_call(grid_kernel, grid=(SLOTS // GROUP,), in_specs=[pl.BlockSpe...  11.1 us

commit v1 on v0

v1 whole, which is shorter than its diff:
```python
import functools

import numpy as np
import jax
import jax.numpy as jnp
import ml_dtypes
from jax import lax
from jax.experimental import pallas as pl
from jax.experimental.pallas import tpu as pltpu
from jax.sharding import PartitionSpec as P

N = 256
TILE = 128
SLOTS = 256
CHIPS = 16
RING = 4
PLANES = 8
GROUP = 32
VMEM_LIMIT = 56 * 1024 * 1024
F32 = jnp.float32
BF16 = jnp.bfloat16


def halves(values):
    high = values.astype(ml_dtypes.bfloat16)
    low = (values - high.astype(np.float64)).astype(ml_dtypes.bfloat16)
    return high, low


def stack(table, axis):
    high, low = halves(table)
    return np.concatenate([high, low, high], axis)


def wave(rows, columns):
    angle = 2.0 * np.pi * (rows[:, None] * columns[None, :] % N) / N
    return np.cos(angle) / 16.0, np.sin(angle) / 16.0


EVEN = 2 * np.arange(TILE)
ODD = (2 * np.arange(TILE) + 1 + TILE) % N


def tables():
    first = np.arange(TILE)
    fwd_right, fwd_left, back_left, back_right = [], [], [], []
    packed = np.arange(2 * TILE).reshape(2, PLANES, 2, 8).transpose(2, 1, 0, 3).reshape(-1)
    for odd in range(2):
        cosine, sine = wave(first, (EVEN, ODD)[odd])
        fwd_right.append(stack(np.block([[cosine, -sine], [sine, cosine]]), 0))
        cosine, sine = wave((EVEN, ODD)[odd], first)
        back_right.append(stack(np.block([[cosine, sine], [-sine, cosine]]), 0))
        cosine, sine = wave(first, 2 * first + odd)
        fwd_left.append(stack(np.block([[cosine, sine], [-sine, cosine]]), 1))
        cosine, sine = wave(2 * first + odd, first)
        back_left.append(stack(np.block([[cosine, -sine], [sine, cosine]])[:, packed], 1))
    lanes = []
    cosine, sine = wave(np.arange(N), np.arange(N))
    for chip in range(CHIPS):
        cos_x = np.repeat(cosine[:, chip * 16 : chip * 16 + 16], 8, axis=1)
        sin_x = np.repeat(sine[:, chip * 16 : chip * 16 + 16], 8, axis=1)
        cos_parts, sin_parts = halves(cos_x), halves(sin_x)
        lanes.append(np.concatenate([cos_parts[0], sin_parts[0], cos_parts[1], sin_parts[1]], 1))
    phases = np.stack(lanes)
    lane = np.arange(TILE)
    order = np.stack([np.where(lane < 64, 2 * lane, 2 * lane - TILE + 1), np.where(lane < 64, 2 * lane + 1, 2 * lane - TILE)])
    natural = np.concatenate([np.eye(TILE)[order[0]], np.eye(TILE)[order[1]]], 0).astype(ml_dtypes.bfloat16)
    return {
        "fwd_right": np.stack(fwd_right),
        "fwd_left": np.stack(fwd_left),
        "back_left": np.stack(back_left),
        "back_right": np.stack(back_right),
        "phases": phases,
        "phases_t": np.ascontiguousarray(phases.transpose(0, 2, 1)),
        "natural": natural,
        "packed": np.ascontiguousarray(natural.T),
    }


def split(values):
    high = values.astype(BF16)
    low = (values - high.astype(F32)).astype(BF16)
    return high, low


def dot(a, b):
    return lax.dot_general(a, b, (((1,), (0,)), ((), ())), preferred_element_type=F32)


def wide(values):
    high, low = split(values)
    return jnp.concatenate([high, high, low], 1)


def tall(values):
    high, low = split(values)
    return jnp.concatenate([high, high, low], 0)


def place():
    slab = lax.axis_index("slab")
    core = lax.rem(slab, 2)
    chip = slab // 2
    x, y = lax.rem(chip, RING), chip // RING
    return core, chip, x, y


def device(x, y, core):
    return {"slab": (y * RING + x) * 2 + core}


def up(i, step=1):
    return lax.rem(i + step, RING)


def down(i):
    return lax.rem(i + RING - 1, RING)


def halved(source, target, sem, i, first):
    return [
        pltpu.make_async_copy(source.at[:, i, :, pl.ds(half * TILE, TILE)], target.at[:, i, half], sem.at[i, first + half])
        for half in range(2)
    ]


def meet(peers):
    barrier = pltpu.get_barrier_semaphore()
    for peer in peers:
        pl.semaphore_signal(barrier, inc=1, device_id=peer, device_id_type=pl.DeviceIdType.MESH)
    pl.semaphore_wait(barrier, len(peers))


def remote(src, dst, send, recv, peer):
    return pltpu.make_async_remote_copy(
        src_ref=src, dst_ref=dst, send_sem=send, recv_sem=recv, device_id=peer, device_id_type=pl.DeviceIdType.MESH
    )


class RingSum:
    def __init__(self, src, via_up, via_down, from_down, from_up, send, recv, me, above, below):
        self.src, self.me = src, me
        rows = src.shape[1]
        self.half = (pl.ds(0, rows // 2), pl.ds(rows // 2, rows // 2))
        self.via_up, self.via_down, self.from_down, self.from_up = via_up, via_down, from_down, from_up
        first, second = self.half
        far, near_up, near_down = up(me, 2), up(me), down(me)
        self.copies = [
            remote(src.at[far, first], via_up, send.at[0], recv.at[0], above),
            remote(src.at[far, second], via_down, send.at[1], recv.at[1], below),
            remote(src.at[near_up, second], from_down.at[second], send.at[2], recv.at[2], above),
            remote(src.at[near_down, first], from_up.at[first], send.at[3], recv.at[3], below),
            remote(src.at[near_up, first], from_down.at[first], send.at[4], recv.at[4], above),
            remote(src.at[near_down, second], from_up.at[second], send.at[5], recv.at[5], below),
        ]

    def start_far(self):
        for copy in self.copies[:2]:
            copy.start()

    def start_near(self):
        for copy in self.copies[2:4]:
            copy.start()

    def relay(self):
        first, second = self.half
        self.copies[0].wait_recv()
        near = up(self.me)
        self.src[near, first] = self.src[near, first] + self.via_up[...]
        self.copies[4].start()
        self.copies[1].wait_recv()
        near = down(self.me)
        self.src[near, second] = self.src[near, second] + self.via_down[...]
        self.copies[5].start()

    def finish(self, out):
        for k in (2, 3, 4, 5):
            self.copies[k].wait_recv()
        out[...] = self.src[self.me] + self.from_down[...] + self.from_up[...]

    def drain(self):
        for copy in self.copies:
            copy.wait_send()


def scatter_kernel(
    image, sens, bins, fwd_right, fwd_left, phases, out, bins_row, bins_col, side_out,
    image_buf, sens_buf, field, table, part_a, part_b, mid_a, mid_b,
    va0, va1, va2, va3, vb0, vb1, vb2, vb3, wa0, wa1, wa2, wa3, wb0, wb1, wb2, wb3,
    load_sem, table_sem, bin_send, bin_recv, pair_send, pair_recv, send, recv,
):
    core, chip, x, y = place()
    sibling = device(x, y, 1 - core)
    right, left = device(up(x), y, core), device(down(x), y, core)
    above, below = device(x, up(y), core), device(x, down(y), core)

    def loads(i):
        return halved(image, image_buf, load_sem, i, 0) + halved(sens.at[0], sens_buf, load_sem, i, 2)

    def start_load(i, carry):
        for copy in loads(i):
            copy.start()
        return carry

    lax.fori_loop(0, PLANES, start_load, 0)
    fetch = pltpu.make_async_copy(phases.at[chip], table, table_sem)
    fetch.start()
    bins_row[chip] = jnp.broadcast_to(bins[...].astype(F32), (8, SLOTS))
    others = [{"slab": lax.rem(chip + k, CHIPS) * 2 + core} for k in range(1, CHIPS)]
    meet([sibling] + others)
    spread = [remote(bins_row.at[chip], bins_row.at[chip], bin_send.at[k], bin_recv.at[k], others[k]) for k in range(CHIPS - 1)]
    for copy in spread:
        copy.start()

    def pair(i):
        return remote(field.at[2, i], field.at[core, i], pair_send.at[i], pair_recv.at[i], sibling)

    def plane(i, carry):
        for copy in loads(i):
            copy.wait()
        summed, differed = [], []
        for odd in range(2):
            rows = pl.ds(odd, TILE, stride=2)
            parts = []
            for half in range(2):
                image_re, image_im = image_buf[0, i, half, rows, :], image_buf[1, i, half, rows, :]
                sens_re, sens_im = sens_buf[0, i, half, rows, :], sens_buf[1, i, half, rows, :]
                parts.append((sens_re * image_re - sens_im * image_im, sens_re * image_im + sens_im * image_re))
            summed.append(jnp.concatenate([parts[0][k] + parts[1][k] for k in range(2)], 1))
            differed.append(jnp.concatenate([parts[0][k] - parts[1][k] for k in range(2)], 1))
        even_z = dot(wide(jnp.concatenate(summed, 0)), fwd_right[0])
        odd_z = dot(wide(jnp.concatenate(differed, 0)), fwd_right[1])
        parts = []
        for odd in range(2):
            rows = slice(odd * TILE, (odd + 1) * TILE)
            stacked = jnp.concatenate(
                [
                    jnp.concatenate([even_z[rows, :TILE], odd_z[rows, :TILE]], 1),
                    jnp.concatenate([even_z[rows, TILE:], odd_z[rows, TILE:]], 1),
                ],
                0,
            )
            parts.append(dot(fwd_left[odd], tall(stacked)))
        for side, values in enumerate((parts[0] + parts[1], parts[0] - parts[1])):
            values = values.reshape(2, 8, 2, 8, N)
            for part in range(2):
                field[2 * core, i, pl.ds(8 * side, 8), part] = values[part, :, 0]
                field[2 - core, i, pl.ds(8 * side, 8), part] = values[part, :, 1]
        pair(i).start()
        return carry

    lax.fori_loop(0, PLANES, plane, 0)
    fetch.wait()
    for copy in spread:
        copy.wait_recv()
    bins_col[...] = bins_row[...].reshape(CHIPS * 8, SLOTS).T
    lane = lax.broadcasted_iota(jnp.int32, (SLOTS, TILE), 1)

    def column(p):
        return jnp.sum(jnp.where(lane == 8 * p, bins_col[...], 0.0), axis=1, keepdims=True).astype(jnp.int32)

    side_out[...] = jnp.broadcast_to((column(chip) % 2).astype(F32), (SLOTS, TILE))

    def slab_sums(px, py):
        p = py * RING + px
        bins = column(p)
        kx, ky, side = bins // 16, (bins // 2) % 8, bins % 2
        hot = jnp.where(lax.broadcasted_iota(jnp.int32, (SLOTS, N), 1) == kx, 1.0, 0.0).astype(BF16)
        phase = dot(hot, table[...])
        row = lax.broadcasted_iota(jnp.int32, (SLOTS, 4 * TILE), 1) % 8
        phase = jnp.where(row == ky, phase, 0.0).astype(BF16)
        mats = []
        for k in range(2):
            cosine, sine = phase[:, 2 * k * TILE : (2 * k + 1) * TILE], phase[:, (2 * k + 1) * TILE : (2 * k + 2) * TILE]
            mats.append(jnp.concatenate([jnp.concatenate([cosine, sine], 1), jnp.concatenate([-sine, cosine], 1)], 0))
        rows = jnp.concatenate([field[c, :, p, part].reshape(64, N) for part in range(2) for c in range(2)], 0)
        sums = dot(jnp.concatenate([mats[0], mats[1], mats[0]], 1), tall(rows))
        low_lane = jnp.where(lane < 64, 0, 1) == side
        part_a[px, pl.ds(py * SLOTS, SLOTS)] = jnp.where(low_lane, sums[:SLOTS, :TILE], sums[:SLOTS, TILE:])
        part_b[py, pl.ds(px * SLOTS, SLOTS)] = jnp.where(low_lane, sums[SLOTS:, :TILE], sums[SLOTS:, TILE:])

    def far_column(k, carry):
        slab_sums(up(x, 2), up(y, k))
        return carry

    def far_row(k, carry):
        slab_sums(up(x, 3 + k), up(y, 2))
        return carry

    def near(k, carry):
        m = k + k // 4
        slab_sums(up(x, 3 + m % 3), up(y, 3 + m // 3))
        return carry

    a1 = RingSum(part_a, va0, va1, va2, va3, send.at[0], recv.at[0], x, right, left)
    b1 = RingSum(part_b, vb0, vb1, vb2, vb3, send.at[1], recv.at[1], y, above, below)
    a2 = RingSum(mid_a, wa0, wa1, wa2, wa3, send.at[2], recv.at[2], y, above, below)
    b2 = RingSum(mid_b, wb0, wb1, wb2, wb3, send.at[3], recv.at[3], x, right, left)

    def arrived(i, carry):
        pair(i).wait_recv()
        return carry

    lax.fori_loop(0, PLANES, arrived, 0)
    lax.fori_loop(0, 4, far_column, 0, unroll=2)
    lax.fori_loop(0, 3, far_row, 0, unroll=3)
    a1.start_far()
    b1.start_far()
    lax.fori_loop(0, 8, near, 0, unroll=2)
    a1.start_near()
    b1.start_near()
    slab_sums(x, y)
    a1.relay()
    b1.relay()
    a1.finish(part_a.at[x])
    for k in range(RING):
        mid_a[k] = part_a[x, pl.ds(k * SLOTS, SLOTS)]
    a2.start_far()
    a2.start_near()
    b1.finish(part_b.at[y])
    for k in range(RING):
        mid_b[k] = part_b[y, pl.ds(k * SLOTS, SLOTS)]
    b2.start_far()
    b2.start_near()
    a2.relay()
    b2.relay()
    a2.finish(out.at[0])
    b2.finish(out.at[1])
    for ring in (a1, b1, a2, b2):
        ring.drain()
    for copy in spread:
        copy.wait_send()

    def sent(i, carry):
        pair(i).wait_send()
        return carry

    lax.fori_loop(0, PLANES, sent, 0)


def scatter(image, sens, bins, tab):
    big, small = RING * SLOTS, SLOTS
    vias = []
    for rows in (big, big, small, small):
        vias += [pltpu.VMEM((rows // 2, TILE), F32)] * 2 + [pltpu.VMEM((rows, TILE), F32)] * 2
    vmem = pl.BlockSpec(memory_space=pltpu.VMEM)
    hbm = pl.BlockSpec(memory_space=pl.ANY)
    return pl.pallas_call(
        scatter_kernel,
        out_shape=(
            jax.ShapeDtypeStruct((2, SLOTS, TILE), F32),
            jax.ShapeDtypeStruct((CHIPS, 8, SLOTS), F32),
            jax.ShapeDtypeStruct((SLOTS, CHIPS * 8), F32),
            jax.ShapeDtypeStruct((SLOTS, TILE), F32),
        ),
        in_specs=[hbm, hbm, vmem, vmem, vmem, hbm],
        out_specs=(vmem, vmem, vmem, vmem),
        scratch_shapes=[
            pltpu.VMEM((2, PLANES, 2, N, TILE), F32),
            pltpu.VMEM((2, PLANES, 2, N, TILE), F32),
            pltpu.VMEM((3, PLANES, CHIPS, 2, 8, N), F32),
            pltpu.VMEM((N, 4 * TILE), BF16),
            pltpu.VMEM((RING, big, TILE), F32),
            pltpu.VMEM((RING, big, TILE), F32),
            pltpu.VMEM((RING, small, TILE), F32),
            pltpu.VMEM((RING, small, TILE), F32),
        ]
        + vias
        + [
            pltpu.SemaphoreType.DMA((PLANES, 4)),
            pltpu.SemaphoreType.DMA,
            pltpu.SemaphoreType.DMA((CHIPS - 1,)),
            pltpu.SemaphoreType.DMA((CHIPS - 1,)),
            pltpu.SemaphoreType.DMA((PLANES,)),
            pltpu.SemaphoreType.DMA((PLANES,)),
            pltpu.SemaphoreType.DMA((4, 6)),
            pltpu.SemaphoreType.DMA((4, 6)),
        ],
        compiler_params=pltpu.CompilerParams(collective_id=0, has_side_effects=True, vmem_limit_bytes=VMEM_LIMIT),
    )(image, sens, bins, tab["fwd_right"], tab["fwd_left"], tab["phases"])


def grid_kernel(live, tiles, side, weights, natural, packed, out):
    row = lax.broadcasted_iota(jnp.int32, (32, TILE), 0) % 8
    base = pl.program_id(0) * GROUP
    for g in range(GROUP // 8):
        rows = pl.ds(8 * g, 8)
        upper = jnp.concatenate([side[rows]] * 4, 0) == 1.0
        values = jnp.concatenate([tiles[0, rows], tiles[1, rows]], 0)
        high = values.astype(BF16).astype(F32)
        both = jnp.concatenate([high, values - high], 0)
        both = jnp.concatenate([jnp.where(upper, 0.0, both), jnp.where(upper, both, 0.0)], 1).astype(BF16)
        mat = weights[rows].reshape(8 * TILE, TILE)
        spread = lax.dot_general(
            dot(both, natural[...]).astype(BF16), mat, (((1,), (1,)), ((), ())), preferred_element_type=F32
        )
        samples = jnp.zeros((32, TILE), F32)
        for j in range(8):
            samples = jnp.where(row == j, spread[:, j * TILE : (j + 1) * TILE], samples)
        samples = samples[:16] + samples[16:]
        high = samples.astype(BF16).astype(F32)
        both = jnp.concatenate([high, samples - high], 0)
        masked = jnp.concatenate([jnp.where(row == j, both, 0.0).astype(BF16) for j in range(8)], 1)
        back = dot(masked, mat)
        back = back[:16] + back[16:]
        high, low = split(back)
        back = dot(jnp.concatenate([high, low], 0), packed[...])
        back = jnp.where(upper, back[:, TILE:], back[:, :TILE])
        back = back[:16] + back[16:]
        slot = base + 8 * g + lax.broadcasted_iota(jnp.int32, (16, TILE), 0) % 8
        back = jnp.where(slot < live[0], back, 0.0)
        out[0, rows] = back[:8]
        out[1, rows] = back[8:]


def grid(live, tiles, side, weights, tab):
    return pl.pallas_call(
        grid_kernel,
        grid=(SLOTS // GROUP,),
        in_specs=[
            pl.BlockSpec(memory_space=pltpu.SMEM),
            pl.BlockSpec((2, GROUP, TILE), lambda i: (0, i, 0)),
            pl.BlockSpec((GROUP, TILE), lambda i: (i, 0)),
            pl.BlockSpec((GROUP, TILE, TILE), lambda i: (i, 0, 0)),
            pl.BlockSpec((2 * TILE, TILE), lambda i: (0, 0)),
            pl.BlockSpec((TILE, 2 * TILE), lambda i: (0, 0)),
        ],
        out_specs=pl.BlockSpec((2, GROUP, TILE), lambda i: (0, i, 0)),
        out_shape=jax.ShapeDtypeStruct((2, SLOTS, TILE), F32),
        compiler_params=pltpu.CompilerParams(vmem_limit_bytes=VMEM_LIMIT),
    )(live, tiles, side, weights, tab["natural"], tab["packed"])


class RingGather:
    def __init__(self, buf, send, recv, me, above, below):
        rows = buf.shape[1]
        first, second = pl.ds(0, rows // 2), pl.ds(rows // 2, rows // 2)
        near_down, near_up, far = down(me), up(me), up(me, 2)
        self.copies = [
            remote(buf.at[me], buf.at[me], send.at[0], recv.at[0], above),
            remote(buf.at[me], buf.at[me], send.at[1], recv.at[1], below),
            remote(buf.at[near_down, first], buf.at[near_down, first], send.at[2], recv.at[2], above),
            remote(buf.at[near_up, second], buf.at[near_up, second], send.at[3], recv.at[3], below),
        ]

    def start(self):
        self.copies[0].start()
        self.copies[1].start()

    def relay(self):
        self.copies[0].wait_recv()
        self.copies[2].start()
        self.copies[1].wait_recv()
        self.copies[3].start()

    def finish(self):
        self.copies[2].wait_recv()
        self.copies[3].wait_recv()

    def drain(self):
        for copy in self.copies:
            copy.wait_send()


def gather_kernel(
    back, bins_row, bins_col, phases, left, right, sens, out,
    all_a, all_b, mid_a, mid_b, table, sens_buf, plane, outgoing, term, via_up, via_down, from_down, from_up, result,
    local_sem, sens_sem, send, recv, pair_send, pair_recv, coil_send, coil_recv,
):
    core, chip, x, y = place()
    coil = lax.axis_index("coil")
    sibling = device(x, y, 1 - core)
    east, west = device(up(x), y, core), device(down(x), y, core)
    north, south = device(x, up(y), core), device(x, down(y), core)
    over, under = {"coil": up(coil)}, {"coil": down(coil)}
    fetch = pltpu.make_async_copy(phases.at[chip], table, local_sem.at[0])
    fetch.start()

    def load_sens(i, carry):
        for copy in halved(sens.at[0], sens_buf, sens_sem, i, 0):
            copy.start()
        return carry

    lax.fori_loop(0, PLANES, load_sens, 0)
    mid_a[y] = back[0]
    mid_b[x] = back[1]
    meet([sibling, east, west, north, south, over, under])

    a1 = RingGather(mid_a, send.at[0], recv.at[0], y, north, south)
    b1 = RingGather(mid_b, send.at[1], recv.at[1], x, east, west)
    a2 = RingGather(all_a, send.at[2], recv.at[2], x, east, west)
    b2 = RingGather(all_b, send.at[3], recv.at[3], y, north, south)
    a1.start()
    b1.start()
    a1.relay()
    b1.relay()
    a1.finish()
    for k in range(RING):
        all_a[x, pl.ds(k * SLOTS, SLOTS)] = mid_a[k]
    a2.start()
    b1.finish()
    for k in range(RING):
        all_b[y, pl.ds(k * SLOTS, SLOTS)] = mid_b[k]
    b2.start()
    a2.relay()
    b2.relay()
    fetch.wait()
    a2.finish()
    b2.finish()

    def slab_sums(p, carry):
        lane = lax.broadcasted_iota(jnp.int32, (SLOTS, TILE), 1)
        column = jnp.sum(jnp.where(lane == 8 * p, bins_col[...], 0.0), axis=1, keepdims=True).astype(jnp.int32)
        side = column % 2
        bins = bins_row[p, 0:1, :].astype(jnp.int32)
        kx, ky = bins // 16, (bins // 2) % 8
        hot = jnp.where(lax.broadcasted_iota(jnp.int32, (N, SLOTS), 0) == kx, 1.0, 0.0).astype(BF16)
        phase = dot(table[...], hot)
        row = lax.broadcasted_iota(jnp.int32, (4 * TILE, SLOTS), 0) % 8
        phase = jnp.where(row == ky, phase, 0.0).astype(BF16)
        mats = []
        for k in range(2):
            cosine, sine = phase[2 * k * TILE : (2 * k + 1) * TILE], phase[(2 * k + 1) * TILE : (2 * k + 2) * TILE]
            mats.append(jnp.concatenate([jnp.concatenate([cosine, -sine], 1), jnp.concatenate([sine, cosine], 1)], 0))
        px, py = p % RING, p // RING
        tiles = jnp.concatenate([all_a[px, pl.ds(py * SLOTS, SLOTS)], all_b[py, pl.ds(px * SLOTS, SLOTS)]], 0)
        low_lane = jnp.where(lane < 64, 0, 1) == side
        low_lane = jnp.concatenate([low_lane, low_lane], 0)
        tiles = jnp.concatenate([jnp.where(low_lane, tiles, 0.0), jnp.where(low_lane, 0.0, tiles)], 1)
        sums = dot(jnp.concatenate([mats[0], mats[1], mats[0]], 1), tall(tiles))
        sums = sums.reshape(2, 2, PLANES, 8, N)
        lower, upper = sums[:, 0], sums[:, 1]
        mine = jnp.where(core == 0, lower, upper)
        other = jnp.where(core == 0, upper, lower)
        for part in range(2):
            plane[:, core, p, part] = mine[part]
            outgoing[:, p, part] = other[part]
        return carry

    lax.fori_loop(0, CHIPS, slab_sums, 0)
    pair = [remote(outgoing.at[i], plane.at[i, core], pair_send.at[i], pair_recv.at[i], sibling) for i in range(PLANES)]
    for copy in pair:
        copy.start()

    far, near_up, near_down = up(coil, 2), up(coil), down(coil)

    def coil_copies(i):
        s, r = coil_send.at[i], coil_recv.at[i]
        return [
            remote(term.at[i, far, 0], via_up.at[i], s.at[0], r.at[0], over),
            remote(term.at[i, far, 1], via_down.at[i], s.at[1], r.at[1], under),
            remote(term.at[i, near_up, 1], from_down.at[i, 1], s.at[2], r.at[2], over),
            remote(term.at[i, near_down, 0], from_up.at[i, 0], s.at[3], r.at[3], under),
            remote(term.at[i, near_up, 0], from_down.at[i, 0], s.at[4], r.at[4], over),
            remote(term.at[i, near_down, 1], from_up.at[i, 1], s.at[5], r.at[5], under),
        ]

    def relay(i):
        copies = coil_copies(i)
        copies[0].wait_recv()
        term[i, near_up, 0] = term[i, near_up, 0] + via_up[i]
        copies[4].start()
        copies[1].wait_recv()
        term[i, near_down, 1] = term[i, near_down, 1] + via_down[i]
        copies[5].start()

    def plane_back(i, carry):
        remote(outgoing.at[i], plane.at[i, core], pair_send.at[i], pair_recv.at[i], sibling).wait_recv()
        near_half, far_half = plane[i, :, pl.ds(0, 8)], plane[i, :, pl.ds(8, 8)]
        even = dot(left[0], tall((near_half + far_half).reshape(N, N)))
        odd = dot(left[1], tall((near_half - far_half).reshape(N, N)))
        halves_z = []
        for k in range(2):
            lanes = slice(k * TILE, (k + 1) * TILE)
            stacked = jnp.concatenate(
                [jnp.concatenate([v[:TILE, lanes], v[TILE:, lanes]], 1) for v in (even, odd)], 0
            )
            halves_z.append(dot(wide(stacked), right[k]))
        first, second = halves_z[0] + halves_z[1], halves_z[0] - halves_z[1]
        for copy in halved(sens.at[0], sens_buf, sens_sem, i, 0):
            copy.wait()
        for odd in range(2):
            rows = slice(odd * TILE, (odd + 1) * TILE)
            every = pl.ds(odd, TILE, stride=2)
            here = pl.ds(32 * odd, 32)
            for half, values in enumerate((first, second)):
                lanes = pl.ds(half * TILE, TILE)
                field_re, field_im = values[rows, :TILE], values[rows, TILE:]
                sens_re, sens_im = sens_buf[0, i, half, every, :], sens_buf[1, i, half, every, :]
                term[i, :, 0, here, lanes] = (sens_re * field_re + sens_im * field_im).reshape(RING, 32, TILE)
                term[i, :, 1, here, lanes] = (sens_re * field_im - sens_im * field_re).reshape(RING, 32, TILE)
        for copy in coil_copies(i)[:4]:
            copy.start()

        @pl.when(i > 0)
        def _():
            relay(i - 1)

        return carry

    lax.fori_loop(0, PLANES, plane_back, 0)
    relay(PLANES - 1)

    def halved_out(i):
        return [
            pltpu.make_async_copy(result.at[:, i, half], out.at[:, i, :, pl.ds(half * TILE, TILE)], sens_sem.at[i, half])
            for half in range(2)
        ]

    def collect(i, carry):
        copies = coil_copies(i)
        for k in (2, 3, 4, 5):
            copies[k].wait_recv()
        total = term[i, coil] + from_down[i] + from_up[i]
        for part in range(2):
            for odd in range(2):
                for half in range(2):
                    values = total[part, 32 * odd : 32 * odd + 32, half * TILE : (half + 1) * TILE]
                    result[part, i, half, pl.ds(odd, 32, stride=2), :] = values
        for copy in halved_out(i):
            copy.start()
        for copy in copies:
            copy.wait_send()
        return carry

    def stored(i, carry):
        for copy in halved_out(i):
            copy.wait()
        return carry

    lax.fori_loop(0, PLANES, collect, 0)
    lax.fori_loop(0, PLANES, stored, 0)
    for ring in (a1, b1, a2, b2):
        ring.drain()
    for copy in pair:
        copy.wait_send()


def gather(back, bins_row, bins_col, sens, tab):
    quarter = N // RING
    vmem = pl.BlockSpec(memory_space=pltpu.VMEM)
    hbm = pl.BlockSpec(memory_space=pl.ANY)
    return pl.pallas_call(
        gather_kernel,
        out_shape=jax.ShapeDtypeStruct((2, PLANES, quarter, N), F32),
        in_specs=[vmem, vmem, vmem, hbm, vmem, vmem, hbm],
        out_specs=hbm,
        scratch_shapes=[
            pltpu.VMEM((RING, RING * SLOTS, TILE), F32),
            pltpu.VMEM((RING, RING * SLOTS, TILE), F32),
            pltpu.VMEM((RING, SLOTS, TILE), F32),
            pltpu.VMEM((RING, SLOTS, TILE), F32),
            pltpu.VMEM((4 * TILE, N), BF16),
            pltpu.VMEM((2, PLANES, 2, N, TILE), F32),
            pltpu.VMEM((PLANES, 2, CHIPS, 2, 8, N), F32),
            pltpu.VMEM((PLANES, CHIPS, 2, 8, N), F32),
            pltpu.VMEM((PLANES, RING, 2, quarter, N), F32),
            pltpu.VMEM((PLANES, quarter, N), F32),
            pltpu.VMEM((PLANES, quarter, N), F32),
            pltpu.VMEM((PLANES, 2, quarter, N), F32),
            pltpu.VMEM((PLANES, 2, quarter, N), F32),
            pltpu.VMEM((2, PLANES, 2, quarter, TILE), F32),
            pltpu.SemaphoreType.DMA((1,)),
            pltpu.SemaphoreType.DMA((PLANES, 2)),
            pltpu.SemaphoreType.DMA((4, 4)),
            pltpu.SemaphoreType.DMA((4, 4)),
            pltpu.SemaphoreType.DMA((PLANES,)),
            pltpu.SemaphoreType.DMA((PLANES,)),
            pltpu.SemaphoreType.DMA((PLANES, 6)),
            pltpu.SemaphoreType.DMA((PLANES, 6)),
        ],
        compiler_params=pltpu.CompilerParams(collective_id=1, has_side_effects=True, vmem_limit_bytes=VMEM_LIMIT),
    )(back, bins_row, bins_col, tab["phases_t"], tab["back_left"], tab["back_right"], sens)


def body(image, sens, weights, bins, counts):
    tab = {name: jnp.asarray(table) for name, table in tables().items()}
    tiles, bins_row, bins_col, side = scatter(image, sens, bins.reshape(1, SLOTS), tab)
    back = grid(counts, tiles, side, weights, tab)
    return gather(back, bins_row, bins_col, sens, tab)


def solution(mesh):
    in_specs = (
        P(None, "slab", None, None),
        P("coil", None, "slab", None, None),
        P("slab", None, None),
        P("slab"),
        P("slab"),
    )
    out_specs = P(None, "slab", "coil", None)
    return jax.shard_map(body, mesh=mesh, in_specs=in_specs, out_specs=out_specs, check_vma=False)
```

time: 188 us -> 150 us (0.80)
  blocking collectives: 25.8 us -> 0 us
  Pallas kernels: 157 us -> 147 us
    all_gather x1 -> x0, blocking collectives: 25.8 us -> none  [body(): bins_row = lax.all_gather(bins, 'slab').astype(F32)]
    pallas_call x2 -> x1, Pallas kernels: 57.8 us -> 47.5 us  [scatter(): pl.pallas_call(scatter_kernel, out_shape=(jax.ShapeDtypeStruct((2, SLOTS,...]
    pallas_call x1, Pallas kernels: 11.1 us -> 15 us  [grid(): pl.pallas_call(grid_kernel, grid=(SLOTS // GROUP,), in_specs=[pl.BlockSpe...]
    pallas_call x1, Pallas kernels: 87.7 us -> 84.8 us  [gather(): pl.pallas_call(gather_kernel, out_shape=jax.ShapeDtypeStruct((2, PLANES,...]
where the time goes in v1:
time: 150 us
  Pallas kernels  147 us (98%)
  local copies, waits for them, and re-layouts  2.29 us (2%)
    pallas_call x1, Pallas kernels, gather(): pl.pallas_call(gather_kernel, out_shape=jax.ShapeDtypeStruct((2, PLANES,...  84.8 us
    pallas_call x1, Pallas kernels, scatter(): pl.pallas_call(scatter_kernel, out_shape=(jax.ShapeDtypeStruct((2, SLOTS,...  47.5 us
    pallas_call x1, Pallas kernels, grid(): pl.pallas_call(grid_kernel, grid=(SLOTS // GROUP,), in_specs=[pl.BlockSpe...  15 us

profile of v1, /device:TPU:1, one launch (start us, length us, event | category | flops | bytes accessed | tf_op | source)
XLA Modules:
  0.0 150.2 jit_solution(8206199223820729564)
XLA Ops:
  0.7 47.5 %shard_map.127 = (f32[2,256,128]{2,1,0:T(8,128)}, f32[16,8,256]{2,1,0:T(8,128)}, f32[256,128]{1,0:T(8,128)}, f32[256,128]{1,0:T(8,128)}) custom-call(f32[2,8,256,256]{3,2,1,0:T(8,128)} %image.1, f32[1,2,8,256,256]{4,3,2,1,0:T(8,128)} %sens.3, s32[1,256]{1,0:T(1,128)} %bitcast.1, bf16[2,768,256]{2,1,0:T(8,128)(2,1)} %constant.16.clone.fwd_right, ...), custom_call_target="tpu_custom_call" | custom-call | tf_op jit(solution)/shard_map/pallas_call | solution.py:348
  48.1 15.0 %shard_map.128.back = f32[2,256,128]{2,1,0:T(8,128)} custom-call(s32[1]{0:T(128)S(6)} %copy.15.live, f32[2,256,128]{2,1,0:T(8,128)} %get-tuple-element.9.tiles, f32[256,128]{1,0:T(8,128)} %get-tuple-element.10.side, bf16[256,128,128]{2,1,0:T(8,128)(2,1)} %weights.1, bf16[256,128]{1,0:T(8,128)(2,1)} %constant.22.clone.natural, ...), custom_call_target="tpu_custom_call" | custom-call | tf_op jit(solution)/shard_map/pallas_call | solution.py:417
  63.1 84.8 %shard_map.129 = f32[2,8,64,256]{3,2,1,0:T(8,128)} custom-call(f32[2,256,128]{2,1,0:T(8,128)} %shard_map.128.back, f32[16,8,256]{2,1,0:T(8,128)} %get-tuple-element.11.bins_row, f32[256,128]{1,0:T(8,128)} %get-tuple-element.12.bins_col, bf16[16,512,256]{2,1,0:T(8,128)(2,1)} %constant.21.clone.phases, bf16[2,256,768]{2,1,0:T(8,128)(2,1)} %constant.18.clone.left, ...), custom_call_target="tpu_custom_call" | custom-call | tf_op jit(solution)/shard_map/pallas_call | solution.py:643
  147.9 2.3 %copy.16 = f32[2,8,64,256]{3,2,1,0:T(8,128)} copy(f32[2,8,64,256]{3,2,1,0:T(8,128)} %shard_map.129) | data formatting | bytes 2097152
